TPU v7x, 32 devices: a whole 2x2x4 slice. The times are simulated.
32 devices in a mesh: grp: 2 (over y), col: 4 (over z), row: 4 (over x, core).
Axes of the slice: x: 2, y: 2, z: 4, core: 2. Of those that a mesh axis runs over, the one named last changes fastest.
Arguments:
- records: float32 [32768, 1024], P(('grp', 'row'), 'col'), parts along dimension 0, may hold values from -90 to 90
Outputs:
- whitened: float32 [8, 4096, 1024], P(('grp', 'row'), 'col'), parts along dimension 0
There are 2 independent parts, one for each index of `grp`. A program takes and returns all parts, laid end to end along the dimension named above; each array names one. Nothing has to cross between parts.
All inputs are finite; a program needn't handle non-finite values.
Results may differ from a plain program's by a relative error of at most 0.00022.
Values sent between devices are 32-bit elements; how exact they have to be, the bound alone decides.
A program may use at most 64 MiB of HBM per device.

v0:
```python
import jax
import jax.numpy as jnp
from jax import lax
from jax.sharding import PartitionSpec as P

NS_ITERS = 8
TOURS = 2


def shifted(x, axis, by):
    peers = lax.axis_size(axis)
    pairs = [(i, i + by) for i in range(peers) if 0 <= i + by < peers]
    return lax.ppermute(x, axis, pairs)


def product(left, right):
    return jnp.dot(left, right, precision=lax.Precision.HIGHEST, preferred_element_type=jnp.float32)


def local_gram(left, right):
    return lax.dot_general(
        left,
        right,
        (((0,), (0,)), ((), ())),
        precision=lax.Precision.HIGHEST,
        preferred_element_type=jnp.float32,
    )


def inverse_root(gram_pair):
    pair_width = gram_pair.shape[0]
    identity = jnp.eye(pair_width, dtype=jnp.float32)
    norm_total = jnp.sqrt(jnp.sum(gram_pair * gram_pair) + 1e-06)
    root_part = gram_pair / norm_total
    inverse_part = identity
    for repeat in range(NS_ITERS):
        middle = 1.5 * identity - 0.5 * product(inverse_part, root_part)
        root_part = product(root_part, middle)
        inverse_part = product(middle, inverse_part)
    return (inverse_part, norm_total)


def local(records):
    col_count = lax.axis_size("col")
    total_rows = records.shape[0] * lax.axis_size("row")
    position = lax.axis_index("col")
    first_col = position == 0
    last_col = position == col_count - 1
    block_width = records.shape[1] // 2
    pair_cols = records
    for repeat in range(TOURS):
        gram_pair = lax.psum(local_gram(pair_cols, pair_cols), "row")
        inverse_part, norm_total = inverse_root(gram_pair)
        factor = jnp.sqrt(total_rows / norm_total)
        pair_cols = product(pair_cols, inverse_part) * factor
        top_block = pair_cols[:, :block_width]
        bottom_block = pair_cols[:, block_width:]
        moving = repeat + 1 < TOURS
        if not moving:
            moving = True
        outgoing = jnp.where(first_col, bottom_block, top_block)
        arrived = shifted(outgoing, "col", 1)
        returned = shifted(bottom_block, "col", -1)
        new_bottom = jnp.where(last_col, top_block, returned)
        top_block = jnp.where(first_col, top_block, arrived)
        pair_cols = jnp.concatenate([top_block, new_bottom], axis=1)
    spread = lax.all_to_all(pair_cols, "col", split_axis=0, concat_axis=1, tiled=True)
    return spread.reshape(1, spread.shape[0], spread.shape[1])


def solution(mesh):
    placed = (P(("grp", "row"), "col"),)
    return jax.shard_map(
        local, mesh=mesh, in_specs=placed, out_specs=P(("grp", "row"), "col", None), check_vma=False
    )
```

profile of v0, /device:TPU:0, one launch (start us, length us, event | category | flops | bytes accessed | tf_op | source)
XLA Modules:
  0.0 348.7 jit_solution(7640274950284962269)
XLA Ops:
  6.5 10.9 %fusion.8 = f32[256,256]{1,0:T(8,128)} fusion(f32[4096,256]{1,0:T(8,128)} %param.1), kind=kOutput, calls=%fused_computation.56 | convolution fusion | flops 3221225472 | bytes 4456448 | tf_op jit(solution)/shard_map/dot_general | solution.py:21
  17.7 34.6 %all-reduce.3.cloned.1.call-done = f32[256,256]{1,0:T(8,128)} async-done(((f32[256,256]{1,0:T(8,128)}), f32[256,256]{1,0:T(8,128)}) %all-reduce.3.cloned.1.call-update) | async-done | bytes 262160 | tf_op jit(solution)/shard_map/psum | solution.py:52
  52.3 1.6 multiply_reduce_fusion.1
  54.6 1.3 select_subtract_fusion.15
  56.2 1.3 fusion.4
  57.5 0.4 select_subtract_fusion.14
  57.9 0.4 fusion.10
  58.3 0.4 fusion.9
  58.7 0.4 select_subtract_fusion.13
  59.1 0.4 fusion.12
  59.5 0.4 fusion.11
  59.8 0.4 select_subtract_fusion.12
  60.6 0.4 fusion.13
  61.0 0.4 select_subtract_fusion.11
  61.4 0.4 fusion.16
  61.8 0.4 fusion.15
  62.2 0.4 select_subtract_fusion.10
  62.6 0.4 fusion.18
  62.9 0.4 fusion.17
  63.3 0.4 select_subtract_fusion.9
  63.7 0.4 fusion.19
  64.6 0.4 select_subtract_fusion.8
  65.0 0.4 fusion.21
  65.4 8.8 %fusion = f32[4096,256]{0,1:T(8,128)S(1)} fusion(f32[256,256]{1,0:T(8,128)S(1)} %fusion.21, f32[4096,256]{1,0:T(8,128)} %param.1, f32[]{:T(128)S(6)} %sqrt.13), kind=kOutput, calls=%fused_computation.2 | convolution fusion | flops 3222274048 | bytes 8650756 | tf_op jit(solution)/shard_map/dot_general | solution.py:17
  74.1 2.4 slice_select_fusion.5
  76.6 0.8 copy-done
  77.4 3.5 %collective-permute-start = (f32[4096,128]{0,1:T(8,128)}, f32[4096,128]{0,1:T(8,128)S(1)}, u32[]{:S(2)}, u32[]{:S(2)}) collective-permute-start(f32[4096,128]{0,1:T(8,128)} %get-tuple-element.11), channel_id=1, source_target_pairs={{0,4},{4,8},{8,12},{1,5},{5,9},{9,13},{2,6},{6,10},{10,14},{3,7},{... | collective-permute-start | bytes 6291464 | tf_op jit(solution)/shard_map/ppermute | solution.py:13
  80.9 1.5 collective-permute-start.1
  82.4 42.4 %collective-permute-done = f32[4096,128]{0,1:T(8,128)S(1)} collective-permute-done((f32[4096,128]{0,1:T(8,128)}, f32[4096,128]{0,1:T(8,128)S(1)}, u32[]{:S(2)}, u32[]{:S(2)}) %collective-permute-start) | collective-permute-done | bytes 2097184 | tf_op jit(solution)/shard_map/ppermute | solution.py:13
  124.9 1.3 copy-done.2
  126.2 2.9 collective-permute-done.1
  129.1 2.6 slice_select_fusion.4
  131.7 1.3 copy-done.1
  133.1 4.2 %fusion.1 = f32[256,256]{1,0:T(8,128)} fusion(f32[4096,128]{0,1:T(8,128)S(1)} %get-tuple-element.10, f32[4096,128]{0,1:T(8,128)S(1)} %get-tuple-element.9), kind=kOutput, calls=%fused_computation.6 | convolution fusion | flops 3222274048 | bytes 4456448 | tf_op jit(solution)/shard_map/dot_general | solution.py:21
  137.3 32.0 %all-reduce.5.cloned.1.call-done = f32[256,256]{1,0:T(8,128)} async-done(((f32[256,256]{1,0:T(8,128)}), f32[256,256]{1,0:T(8,128)}) %all-reduce.5.cloned.1.call-update) | async-done | bytes 262160 | tf_op jit(solution)/shard_map/psum | solution.py:52
  169.3 1.6 multiply_reduce_fusion
  171.7 1.3 select_subtract_fusion.7
  173.2 1.3 fusion.5
  174.6 0.4 select_subtract_fusion.6
  175.0 0.4 fusion.23
  175.3 0.4 fusion.22
  175.7 0.4 select_subtract_fusion.5
  176.1 0.4 fusion.25
  176.5 0.4 fusion.24
  176.9 0.4 select_subtract_fusion.4
  177.3 0.4 fusion.27
  178.1 0.4 select_subtract_fusion.3
  178.8 0.4 fusion.28
  179.2 0.4 select_subtract_fusion.2
  179.6 0.4 fusion.31
  180.4 0.4 select_subtract_fusion.1
  181.2 0.4 fusion.33
  181.6 0.6 select_subtract_fusion
  182.2 0.4 fusion.34
  182.6 5.9 %convolution_multiply_fusion = f32[4096,256]{0,1:T(8,128)S(1)} fusion(f32[256,256]{1,0:T(8,128)S(1)} %fusion.34, f32[4096,128]{0,1:T(8,128)} %copy-done.1, f32[4096,128]{0,1:T(8,128)S(1)} %get-tuple-element.9, f32[]{:T(128)S(6)} %sqrt.15), kind=kOutput, calls=%fused_computation | convolution fusion | flops 3223322624 | bytes 8650756 | tf_op jit(solution)/shard_map/dot_general | solution.py:17
  188.5 0.4 slice_select_fusion.2
  188.9 3.5 %collective-permute-start.2 = (f32[4096,128]{0,1:T(8,128)S(1)}, f32[4096,128]{0,1:T(8,128)S(1)}, u32[]{:S(2)}, u32[]{:S(2)}) collective-permute-start(f32[4096,128]{0,1:T(8,128)S(1)} %get-tuple-element.7), channel_id=1, source_target_pairs={{0,4},{4,8},{8,12},{1,5},{5,9},{9,13},{2,6},{6,10},{10,14},{3,7},{... | collective-permute-start | bytes 6291464 | tf_op jit(solution)/shard_map/ppermute | solution.py:13
  192.5 1.3 collective-permute-start.3
  193.8 42.3 %collective-permute-done.2 = f32[4096,128]{0,1:T(8,128)S(1)} collective-permute-done((f32[4096,128]{0,1:T(8,128)S(1)}, f32[4096,128]{0,1:T(8,128)S(1)}, u32[]{:S(2)}, u32[]{:S(2)}) %collective-permute-start.2) | collective-permute-done | bytes 2097184 | tf_op jit(solution)/shard_map/ppermute | solution.py:13
  236.1 4.2 %collective-permute-done.3 = f32[4096,128]{0,1:T(8,128)S(1)} collective-permute-done((f32[4096,128]{0,1:T(8,128)S(1)}, f32[4096,128]{0,1:T(8,128)S(1)}, u32[]{:S(2)}, u32[]{:S(2)}) %collective-permute-start.3) | collective-permute-done | bytes 2097184 | tf_op jit(solution)/shard_map/ppermute | solution.py:13
  240.3 0.5 slice_select_fusion.1
  240.9 0.4 pad_maximum_fusion.1
  241.6 94.5 %all_to_all.16 = f32[4,1024,256]{1,2,0:T(8,128)} all-to-all(f32[4,1024,256]{1,2,0:T(8,128)S(1)} %bitcast.99), channel_id=1, replica_groups=mesh['grp'=2,'col'=4,'row'=4] {'col'}, dimensions={0} | all-to-all | bytes 8388608 | tf_op jit(solution)/shard_map/all_to_all | solution.py:67
  336.1 5.3 %copy.4 = f32[1,1024,1024]{2,1,0:T(8,128)} copy(f32[1,1024,1024]{1,2,0:T(8,128)} %bitcast.100) | data formatting | bytes 8388608 | tf_op jit(solution)/shard_map/reshape | solution.py:68
  (16 shorter events, 3.4 us)
Async XLA Ops:
  6.5 45.8 %all-reduce.3.cloned.1.call-start = ((), (), s32[]{:S(2)}) async-start(), calls=%async_computation.1 | async-start | bytes 524288 | tf_op jit(solution)/shard_map/psum | solution.py:52
  17.5 151.8 %all-reduce.5.cloned.1.call-start = ((), (), s32[]{:S(2)}) async-start(), calls=%async_computation.2 | async-start | bytes 524288 | tf_op jit(solution)/shard_map/psum | solution.py:52
  74.1 3.3 copy-start
  77.4 47.4 %collective-permute-start = (f32[4096,128]{0,1:T(8,128)}, f32[4096,128]{0,1:T(8,128)S(1)}, u32[]{:S(2)}, u32[]{:S(2)}) collective-permute-start(f32[4096,128]{0,1:T(8,128)} %get-tuple-element.11), channel_id=1, source_target_pairs={{0,4},{4,8},{8,12},{1,5},{5,9},{9,13},{2,6},{6,10},{10,14},{3,7},{... | collective-permute-start | bytes 6291464 | tf_op jit(solution)/shard_map/ppermute | solution.py:13
  80.9 48.2 %collective-permute-start.1 = (f32[4096,128]{0,1:T(8,128)}, f32[4096,128]{0,1:T(8,128)}, u32[]{:S(2)}, u32[]{:S(2)}) collective-permute-start(f32[4096,128]{0,1:T(8,128)} %get-tuple-element.12), channel_id=1, source_target_pairs={{4,0},{8,4},{12,8},{5,1},{9,5},{13,9},{6,2},{10,6},{14,10},{7,3},{... | collective-permute-start | bytes 6291464 | tf_op jit(solution)/shard_map/ppermute | solution.py:13
  124.8 1.3 copy-start.2
  131.7 1.3 copy-start.1
  188.9 47.1 %collective-permute-start.2 = (f32[4096,128]{0,1:T(8,128)S(1)}, f32[4096,128]{0,1:T(8,128)S(1)}, u32[]{:S(2)}, u32[]{:S(2)}) collective-permute-start(f32[4096,128]{0,1:T(8,128)S(1)} %get-tuple-element.7), channel_id=1, source_target_pairs={{0,4},{4,8},{8,12},{1,5},{5,9},{9,13},{2,6},{6,10},{10,14},{3,7},{... | collective-permute-start | bytes 6291464 | tf_op jit(solution)/shard_map/ppermute | solution.py:13
  192.5 47.9 %collective-permute-start.3 = (f32[4096,128]{0,1:T(8,128)S(1)}, f32[4096,128]{0,1:T(8,128)S(1)}, u32[]{:S(2)}, u32[]{:S(2)}) collective-permute-start(f32[4096,128]{0,1:T(8,128)S(1)} %get-tuple-element.8), channel_id=1, source_target_pairs={{4,0},{8,4},{12,8},{5,1},{9,5},{13,9},{6,2},{10,6},{14,10},{7,3},{... | collective-permute-start | bytes 6291464 | tf_op jit(solution)/shard_map/ppermute | solution.py:13
Sparse Core Ops, SparseCore 0:
  17.6 34.6 all-reduce.2
  137.4 31.8 all-reduce.4
where the time goes:
time: 354 us; the launch traced here: 349 us
  waiting for transfers between devices  159 us (45%)
  blocking collectives  94.5 us (27%)
  matrix products  51 us (14%)
  between operations  15.9 us (4%)
  starting transfers between devices  10 us (3%)
  other arithmetic  9.72 us (3%)
  local copies, waits for them, and re-layouts  9.11 us (3%)
    all_to_all x1, blocking collectives, local(): lax.all_to_all(pair_cols, 'col', split_axis=0, concat_axis=1, tiled=True)  94.5 us
    ppermute x4, waiting for transfers between devices, shifted(): return lax.ppermute(x, axis, pairs)  91.9 us
    psum x2, waiting for transfers between devices, local(): gram_pair = lax.psum(local_gram(pair_cols, pair_cols), 'row')  66.6 us
    dot_general x48, matrix products, product(): jnp.dot(left, right, precision=lax.Precision.HIGHEST, preferred_element_t...  35.8 us
    dot_general x2, matrix products, local_gram(): lax.dot_general(left, right, (((0,), (0,)), ((), ())), precision=lax.Prec...  15.2 us
    ppermute x4, starting transfers between devices, shifted(): return lax.ppermute(x, axis, pairs)  9.83 us
  transfers between devices with their start and end apart: 6, of which 6 were waited for; matrix products, arithmetic and copies ran while one was open for 0% of the time, Pallas kernels for 0%

commit v1 on v0

v1 whole, which is shorter than its diff:
```python
import jax
import jax.numpy as jnp
from jax import lax
from jax.experimental import pallas as pl
from jax.experimental.pallas import tpu as pltpu
from jax.sharding import PartitionSpec as P

NS_ITERS = 8
TOURS = 2
MESH = pl.DeviceIdType.MESH
F32 = jnp.float32
BF16 = jnp.bfloat16
ROWS_FIRST = (((0,), (0,)), ((), ()))
PLAIN = (((1,), (0,)), ((), ()))
SLOTS = (((0, 0), (1, 1)), ((0, 1), (2, 1)), ((1, 0), (3, 1)), ((2, 0), (3, 0)))
PLACES = ((0, 2), (4, 1), (6, 3), (7, 5))


def exact_dot(left, right):
    return jnp.dot(left, right, precision=lax.Precision.HIGHEST, preferred_element_type=F32)


def halves_of(value):
    high = value.astype(BF16)
    low = (value - high.astype(F32)).astype(BF16)
    return high, low


def split_dot(left, right, dims=PLAIN):
    left_high, left_low = left
    right_high, right_low = right

    def one(a, b):
        return lax.dot_general(a, b, dims, preferred_element_type=F32)

    return one(left_high, right_high) + (one(left_high, right_low) + one(left_low, right_high))


def identity_of(width):
    rows = lax.broadcasted_iota(jnp.int32, (width, width), 0)
    cols = lax.broadcasted_iota(jnp.int32, (width, width), 1)
    return jnp.where(rows == cols, 1.0, 0.0).astype(F32)


def norm_of(gram):
    total = jnp.sum(jnp.sum(gram * gram, axis=1, keepdims=True), axis=0, keepdims=True)
    return jnp.sqrt(total + 1e-06)


def newton(y_ref, z_ref, count):
    width = y_ref.shape[1]
    identity = identity_of(width)
    for i in range(count):
        middle = 1.5 * identity - 0.5 * y_ref[i]
        y_ref[i] = exact_dot(y_ref[i], middle)
        z_ref[i] = middle

    @pl.loop(1, NS_ITERS - 1)
    def _(step):
        middles = []
        for i in range(count):
            middles.append(1.5 * identity - 0.5 * exact_dot(z_ref[i], y_ref[i]))
        for i in range(count):
            y_ref[i] = exact_dot(y_ref[i], middles[i])
            z_ref[i] = exact_dot(middles[i], z_ref[i])

    for i in range(count):
        middle = 1.5 * identity - 0.5 * exact_dot(z_ref[i], y_ref[i])
        z_ref[i] = exact_dot(middle, z_ref[i])


def kernel(x_ref, out_ref, w, got, ex, g, ga, sb, gb, gf, y1, z1, dg, dq, df, part, rs, zb, cq, cf, y2, z2,
           send_sem, recv_sem):
    n_col, n_row = 4, 4
    c = lax.axis_index("col")
    r = lax.axis_index("row")
    slab, width = x_ref.shape
    half = width // 2
    rows = slab // n_col
    quarter = half // n_row
    total_rows = float(slab * n_row)

    def col_peer(k):
        return {"col": lax.rem(c + k, n_col)}

    def row_peer(k):
        return {"row": lax.rem(r + k, n_row)}

    def remote(src, dst, sem, device):
        copy = pltpu.make_async_remote_copy(
            src_ref=src, dst_ref=dst, send_sem=send_sem.at[sem], recv_sem=recv_sem.at[sem],
            device_id=device, device_id_type=MESH)
        copy.start()
        return copy

    barrier = pltpu.get_barrier_semaphore()
    for k in range(1, n_row):
        pl.semaphore_signal(barrier, inc=1, device_id=row_peer(k), device_id_type=MESH)
    for k in range(1, n_col):
        pl.semaphore_signal(barrier, inc=1, device_id=col_peer(k), device_id_type=MESH)

    tile = 512
    g[...] = jnp.zeros_like(g)

    @pl.loop(0, slab // tile)
    def _(t):
        piece = halves_of(x_ref[pl.ds(pl.multiple_of(t * tile, tile), tile), :])
        g[...] += split_dot(piece, piece, ROWS_FIRST)

    pl.semaphore_wait(barrier, n_row + n_col - 2)

    core = lax.rem(r, 2)
    mine = pl.ds(pl.multiple_of(core * half, half), half)
    other = pl.ds(pl.multiple_of((1 - core) * half, half), half)
    core_peer = {"row": r + 1 - 2 * core}
    copy = remote(g.at[other], ga, 0, core_peer)
    copy.wait()
    sb[...] = g[mine, :] + ga[...]
    copy = remote(sb, gb, 1, row_peer(2))
    copy.wait()
    gf[mine, :] = sb[...] + gb[...]
    copy = remote(gf.at[mine], gf.at[mine], 2, core_peer)
    copy.wait()

    norm = norm_of(gf[...])
    y1[0] = gf[...] / norm
    newton(y1, z1, 1)
    z1[0] = z1[0] * jnp.sqrt(total_rows / norm)

    odd = lax.rem(c, 2)
    side = c // 2
    hx = 1 - odd * (1 - side)
    ho = 1 - hx
    partner = c + 1 - 2 * odd
    partner_far = lax.rem(partner + 2, n_col)
    far = lax.rem(c + 2, n_col)
    far_other = lax.rem(partner + 2, n_col)

    def chunk(j):
        return pl.ds(pl.multiple_of(j * rows, rows), rows)

    piece_rows = min(256, rows)

    def rotate(j):
        @pl.loop(0, rows // piece_rows)
        def _(t):
            at = pl.ds(pl.multiple_of(j * rows + t * piece_rows, piece_rows), piece_rows)
            turned = split_dot(halves_of(x_ref[at, :]), halves_of(z1[0]))
            w[0, at, :] = turned[:, :half]
            w[1, at, :] = turned[:, half:]

    first = []
    for k in (2, 3, 1):
        j = lax.rem(c + k, n_col)
        rotate(j)
        first.append(remote(w.at[hx, chunk(j)], got.at[c, hx], 2 + k, {"col": j}))
    first.append(remote(w.at[ho, chunk(partner)], got.at[c, ho], 6, {"col": partner}))
    first.append(remote(w.at[ho, chunk(partner_far)], ex.at[odd], 7, {"col": partner}))

    turned_gram = exact_dot(exact_dot(z1[0], gf[...]), z1[0])
    dg[0] = turned_gram[:half, :half]
    dg[1] = turned_gram[half:, half:]
    strip = pl.ds(pl.multiple_of(r * quarter, quarter), quarter)
    diagonal = []
    for k in (1, 2, 3):
        diagonal.append(remote(dg.at[:, strip], dq.at[c], 7 + k, col_peer(k)))
    dq[c] = dg[:, strip, :]

    rotate(c)
    got[c, 0] = w[0, chunk(c), :]
    got[c, 1] = w[1, chunk(c), :]
    ex[odd] = w[ho, chunk(far), :]

    for copy in diagonal:
        copy.wait()
    for k in (1, 2, 3):
        diagonal.append(remote(dq, df.at[r], 10 + k, row_peer(k)))
    df[r] = dq[...]
    for copy in diagonal[3:]:
        copy.wait()

    for copy in first:
        copy.wait_send()
    second = [
        remote(w.at[ho, chunk(far)], got.at[c, ho], 14, {"col": far}),
        remote(w.at[ho, chunk(far_other)], got.at[c, ho], 15, {"col": far_other}),
    ]
    for copy in first:
        copy.wait_recv()

    def cross(left, right):
        return split_dot(halves_of(left), halves_of(right), ROWS_FIRST)

    left_col = 2 * side
    part[...] = jnp.zeros_like(part)

    @pl.loop(0, rows // piece_rows)
    def _(t):
        at = pl.ds(pl.multiple_of(t * piece_rows, piece_rows), piece_rows)
        part[0] += cross(got[0, 1, at, :], got[2, 1, at, :])
        part[1] += cross(got[1, 0, at, :], got[3, 1, at, :])
        part[2] += cross(got[left_col, 0, at, :], got[left_col + 1, 1 - side, at, :])
        part[2] += cross(ex[0, at, :], ex[1, at, :])

    copies = []
    for k in (1, 2, 3):
        q = lax.rem(r + k, n_row)
        theirs = pl.ds(pl.multiple_of(q * quarter, quarter), quarter)
        copies.append(remote(part.at[:, theirs], rs.at[k - 1], 15 + k, {"row": q}))
    for copy in copies:
        copy.wait()
    zb[c] = (part[:, strip, :] + rs[0]) + (rs[1] + rs[2])
    copies = [remote(zb.at[c], zb.at[c], 18 + k, col_peer(k)) for k in (1, 2, 3)]
    for copy in copies:
        copy.wait()
    cq[0] = zb[0, 2] + zb[1, 2]
    cq[1] = (zb[0, 0] + zb[1, 0]) + (zb[2, 0] + zb[3, 0])
    cq[2] = (zb[0, 1] + zb[1, 1]) + (zb[2, 1] + zb[3, 1])
    cq[3] = zb[2, 2] + zb[3, 2]
    copies = [remote(cq, cf.at[r], 21 + k, row_peer(k)) for k in (1, 2, 3)]
    cf[r] = cq[...]
    for copy in copies:
        copy.wait()

    factors = []
    for slot, ((lc, lh), (rc, rh)) in enumerate(SLOTS):
        for q in range(n_row):
            at = slice(q * quarter, (q + 1) * quarter)
            low = slice(half + q * quarter, half + (q + 1) * quarter)
            y2[slot, at, :half] = df[q, lc, lh]
            y2[slot, low, half:] = df[q, rc, rh]
            y2[slot, at, half:] = cf[q, slot]
        y2[slot, half:, :half] = jnp.transpose(y2[slot, :half, half:])
        gram = y2[slot]
        norm = norm_of(gram)
        y2[slot] = gram / norm
        factors.append(jnp.sqrt(total_rows / norm))
    newton(y2, z2, 4)
    for slot in range(4):
        z2[slot] = z2[slot] * factors[slot]

    def finish(slot):
        (lc, lh), (rc, rh) = SLOTS[slot]

        @pl.loop(0, rows // piece_rows)
        def _(t):
            at = pl.ds(pl.multiple_of(t * piece_rows, piece_rows), piece_rows)
            both = jnp.concatenate([got[lc, lh, at, :], got[rc, rh, at, :]], axis=1)
            turned = split_dot(halves_of(both), halves_of(z2[slot]))
            for side_of in range(2):
                place = PLACES[slot][side_of]
                out_ref[at, place * half:(place + 1) * half] = turned[:, side_of * half:(side_of + 1) * half]

    finish(1)
    finish(2)
    for copy in second:
        copy.wait()
    finish(0)
    finish(3)


def fused(records):
    slab, width = records.shape
    half = width // 2
    rows = slab // 4
    quarter = half // 4
    out = pl.pallas_call(
        kernel,
        out_shape=jax.ShapeDtypeStruct((rows, 4 * width), F32),
        in_specs=[pl.BlockSpec(memory_space=pltpu.VMEM)],
        out_specs=pl.BlockSpec(memory_space=pltpu.VMEM),
        scratch_shapes=[
            pltpu.VMEM((2, slab, half), F32),
            pltpu.VMEM((4, 2, rows, half), F32),
            pltpu.VMEM((2, rows, half), F32),
            pltpu.VMEM((width, width), F32),
            pltpu.VMEM((half, width), F32),
            pltpu.VMEM((half, width), F32),
            pltpu.VMEM((half, width), F32),
            pltpu.VMEM((width, width), F32),
            pltpu.VMEM((1, width, width), F32),
            pltpu.VMEM((1, width, width), F32),
            pltpu.VMEM((2, half, half), F32),
            pltpu.VMEM((4, 2, quarter, half), F32),
            pltpu.VMEM((4, 4, 2, quarter, half), F32),
            pltpu.VMEM((3, half, half), F32),
            pltpu.VMEM((3, 3, quarter, half), F32),
            pltpu.VMEM((4, 3, quarter, half), F32),
            pltpu.VMEM((4, quarter, half), F32),
            pltpu.VMEM((4, 4, quarter, half), F32),
            pltpu.VMEM((4, width, width), F32),
            pltpu.VMEM((4, width, width), F32),
            pltpu.SemaphoreType.DMA((25,)),
            pltpu.SemaphoreType.DMA((25,)),
        ],
        compiler_params=pltpu.CompilerParams(
            collective_id=0, has_side_effects=True, vmem_limit_bytes=48 * 1024 * 1024),
    )(records)
    return out.reshape(1, rows, 4 * width)


def shifted(x, axis, by):
    peers = lax.axis_size(axis)
    pairs = [(i, i + by) for i in range(peers) if 0 <= i + by < peers]
    return lax.ppermute(x, axis, pairs)


def local_gram(left, right):
    return lax.dot_general(
        left, right, ROWS_FIRST, precision=lax.Precision.HIGHEST, preferred_element_type=F32)


def inverse_root(gram_pair):
    identity = jnp.eye(gram_pair.shape[0], dtype=F32)
    norm_total = jnp.sqrt(jnp.sum(gram_pair * gram_pair) + 1e-06)
    root_part = gram_pair / norm_total
    inverse_part = identity
    for repeat in range(NS_ITERS):
        middle = 1.5 * identity - 0.5 * exact_dot(inverse_part, root_part)
        root_part = exact_dot(root_part, middle)
        inverse_part = exact_dot(middle, inverse_part)
    return (inverse_part, norm_total)


def stepwise(records):
    col_count = lax.axis_size("col")
    total_rows = records.shape[0] * lax.axis_size("row")
    position = lax.axis_index("col")
    first_col = position == 0
    last_col = position == col_count - 1
    block_width = records.shape[1] // 2
    pair_cols = records
    for repeat in range(TOURS):
        gram_pair = lax.psum(local_gram(pair_cols, pair_cols), "row")
        inverse_part, norm_total = inverse_root(gram_pair)
        factor = jnp.sqrt(total_rows / norm_total)
        pair_cols = exact_dot(pair_cols, inverse_part) * factor
        top_block = pair_cols[:, :block_width]
        bottom_block = pair_cols[:, block_width:]
        outgoing = jnp.where(first_col, bottom_block, top_block)
        arrived = shifted(outgoing, "col", 1)
        returned = shifted(bottom_block, "col", -1)
        new_bottom = jnp.where(last_col, top_block, returned)
        top_block = jnp.where(first_col, top_block, arrived)
        pair_cols = jnp.concatenate([top_block, new_bottom], axis=1)
    spread = lax.all_to_all(pair_cols, "col", split_axis=0, concat_axis=1, tiled=True)
    return spread.reshape(1, spread.shape[0], spread.shape[1])


def solution(mesh):
    placed = (P(("grp", "row"), "col"),)
    small = mesh.shape["col"] == 4 and mesh.shape["row"] == 4
    return jax.shard_map(
        fused if small else stepwise,
        mesh=mesh, in_specs=placed, out_specs=P(("grp", "row"), "col", None), check_vma=False
    )
```

time: 354 us -> 174 us (0.49); the launches traced: 349 us -> 174 us
  Pallas kernels: 0 us -> 172 us
  waiting for transfers between devices: 159 us -> 0 us
  blocking collectives: 94.5 us -> 0 us
  matrix products: 51 us -> 0 us
  between operations: 15.9 us -> 0.01 us
  starting transfers between devices: 10 us -> 0 us
  other arithmetic: 9.72 us -> 0 us
  local copies, waits for them, and re-layouts: 9.11 us -> 2.02 us
    pallas_call x0 -> x1, Pallas kernels: none -> 172 us  [fused(): pl.pallas_call(kernel, out_shape=jax.ShapeDtypeStruct((rows, 4 * width),...]
    all_to_all x1 -> x0, blocking collectives: 94.5 us -> none  [local(): lax.all_to_all(pair_cols, 'col', split_axis=0, concat_axis=1, tiled=True)]
    ppermute x4 -> x0, waiting for transfers between devices: 91.9 us -> none  [shifted(): return lax.ppermute(x, axis, pairs)]
    psum x2 -> x0, waiting for transfers between devices: 66.6 us -> none  [local(): gram_pair = lax.psum(local_gram(pair_cols, pair_cols), 'row')]
    dot_general x50 -> x0, matrix products: 51 us -> none  [the longest x48 35.8 us: product(): jnp.dot(left, right, precision=lax.Precision.HIGHEST, preferred_element_t...]
    ppermute x4 -> x0, starting transfers between devices: 9.83 us -> none  [shifted(): return lax.ppermute(x, axis, pairs)]
    select_n x4 -> x0, other arithmetic: 6.02 us -> none  [the longest x2 3.15 us: local(): top_block = jnp.where(first_col, top_block, arrived)]
    reshape x1 -> x0, local copies, waits for them, and re-layouts: 5.34 us -> none  [local(): return spread.reshape(1, spread.shape[0], spread.shape[1])]
  transfers between devices with their start and end apart: 6 -> 0, of which waited for: 6 -> 0; matrix products, arithmetic and copies ran while one was open for 0% -> 0% of each run, Pallas kernels for 0% -> 0%
where the time goes in v1:
time: 174 us
  Pallas kernels  172 us (99%)
  local copies, waits for them, and re-layouts  2.02 us (1%)
    pallas_call x1, Pallas kernels, fused(): pl.pallas_call(kernel, out_shape=jax.ShapeDtypeStruct((rows, 4 * width),...  172 us

profile of v1, /device:TPU:0, one launch (start us, length us, event | category | flops | bytes accessed | tf_op | source)
XLA Modules:
  0.0 173.5 jit_solution(3165654213866576977)
XLA Ops:
  0.0 171.5 %shard_map.17 = f32[1024,1024]{1,0:T(8,128)S(1)} custom-call(f32[4096,256]{1,0:T(8,128)} %x_ref.1), custom_call_target="tpu_custom_call" | custom-call | tf_op jit(solution)/shard_map/pallas_call | solution.py:267
  171.5 2.0 %copy.3 = f32[1,1024,1024]{2,1,0:T(8,128)} copy(f32[1,1024,1024]{2,1,0:T(8,128)S(1)} %bitcast.1) | data formatting | bytes 8388608

commit v2 on v1

--- a/solution.py
+++ b/solution.py
@@ -101,11 +101,15 @@
 
     tile = 512
     g[...] = jnp.zeros_like(g)
+    gf[...] = jnp.zeros_like(gf)
 
     @pl.loop(0, slab // tile)
     def _(t):
         piece = halves_of(x_ref[pl.ds(pl.multiple_of(t * tile, tile), tile), :])
-        g[...] += split_dot(piece, piece, ROWS_FIRST)
+        g[...] += lax.dot_general(piece[0], piece[0], ROWS_FIRST, preferred_element_type=F32)
+        gf[...] += lax.dot_general(piece[0], piece[1], ROWS_FIRST, preferred_element_type=F32)
+
+    g[...] += gf[...] + jnp.transpose(gf[...])
 
     pl.semaphore_wait(barrier, n_row + n_col - 2)
 
@@ -132,7 +136,6 @@
     hx = 1 - odd * (1 - side)
     ho = 1 - hx
     partner = c + 1 - 2 * odd
-    partner_far = lax.rem(partner + 2, n_col)
     far = lax.rem(c + 2, n_col)
     far_other = lax.rem(partner + 2, n_col)
 
@@ -149,13 +152,8 @@
             w[0, at, :] = turned[:, :half]
             w[1, at, :] = turned[:, half:]
 
-    first = []
-    for k in (2, 3, 1):
-        j = lax.rem(c + k, n_col)
-        rotate(j)
-        first.append(remote(w.at[hx, chunk(j)], got.at[c, hx], 2 + k, {"col": j}))
-    first.append(remote(w.at[ho, chunk(partner)], got.at[c, ho], 6, {"col": partner}))
-    first.append(remote(w.at[ho, chunk(partner_far)], ex.at[odd], 7, {"col": partner}))
+    rotate(far)
+    crossing = [remote(w.at[hx, chunk(far)], got.at[c, hx], 3, {"col": far})]
 
     turned_gram = exact_dot(exact_dot(z1[0], gf[...]), z1[0])
     dg[0] = turned_gram[:half, :half]
@@ -166,11 +164,31 @@
         diagonal.append(remote(dg.at[:, strip], dq.at[c], 7 + k, col_peer(k)))
     dq[c] = dg[:, strip, :]
 
+    rotate(far_other)
+    crossing.append(remote(w.at[hx, chunk(far_other)], got.at[c, hx], 4, {"col": far_other}))
+    near = [remote(w.at[ho, chunk(far_other)], ex.at[odd], 7, {"col": partner})]
+    rotate(partner)
+    near.append(remote(w.at[hx, chunk(partner)], got.at[c, hx], 5, {"col": partner}))
+    near.append(remote(w.at[ho, chunk(partner)], got.at[c, ho], 6, {"col": partner}))
+
     rotate(c)
     got[c, 0] = w[0, chunk(c), :]
     got[c, 1] = w[1, chunk(c), :]
     ex[odd] = w[ho, chunk(far), :]
 
+    def later(part_of, sem):
+        size = rows // 2
+        sent = []
+        for i, j in enumerate((far, far_other)):
+            at = pl.ds(pl.multiple_of(j * rows + part_of * size, size), size)
+            to = pl.ds(part_of * size, size)
+            sent.append(remote(w.at[ho, at], got.at[c, ho, to], sem + i, {"col": j}))
+        return sent
+
+    for copy in crossing:
+        copy.wait_send()
+    second = later(0, 14)
+
     for copy in diagonal:
         copy.wait()
     for k in (1, 2, 3):
@@ -178,15 +196,10 @@
     df[r] = dq[...]
     for copy in diagonal[3:]:
         copy.wait()
-
-    for copy in first:
-        copy.wait_send()
-    second = [
-        remote(w.at[ho, chunk(far)], got.at[c, ho], 14, {"col": far}),
-        remote(w.at[ho, chunk(far_other)], got.at[c, ho], 15, {"col": far_other}),
-    ]
-    for copy in first:
+    for copy in crossing:
         copy.wait_recv()
+    for copy in near:
+        copy.wait()
 
     def cross(left, right):
         return split_dot(halves_of(left), halves_of(right), ROWS_FIRST)
@@ -211,6 +224,7 @@
         copy.wait()
     zb[c] = (part[:, strip, :] + rs[0]) + (rs[1] + rs[2])
     copies = [remote(zb.at[c], zb.at[c], 18 + k, col_peer(k)) for k in (1, 2, 3)]
+    second += later(1, 25)
     for copy in copies:
         copy.wait()
     cq[0] = zb[0, 2] + zb[1, 2]
@@ -222,7 +236,6 @@
     for copy in copies:
         copy.wait()
 
-    factors = []
     for slot, ((lc, lh), (rc, rh)) in enumerate(SLOTS):
         for q in range(n_row):
             at = slice(q * quarter, (q + 1) * quarter)
@@ -231,13 +244,19 @@
             y2[slot, low, half:] = df[q, rc, rh]
             y2[slot, at, half:] = cf[q, slot]
         y2[slot, half:, :half] = jnp.transpose(y2[slot, :half, half:])
-        gram = y2[slot]
+
+    factors = []
+    for i in range(2):
+        gram = y2[2 * core + i]
         norm = norm_of(gram)
-        y2[slot] = gram / norm
+        y2[2 * core + i] = gram / norm
         factors.append(jnp.sqrt(total_rows / norm))
-    newton(y2, z2, 4)
-    for slot in range(4):
-        z2[slot] = z2[slot] * factors[slot]
+    own = pl.ds(2 * core, 2)
+    newton(y2.at[own], z2.at[own], 2)
+    for i in range(2):
+        z2[2 * core + i] = z2[2 * core + i] * factors[i]
+    copy = remote(z2.at[own], z2.at[own], 27, core_peer)
+    copy.wait()
 
     def finish(slot):
         (lc, lh), (rc, rh) = SLOTS[slot]
@@ -290,8 +309,8 @@
             pltpu.VMEM((4, 4, quarter, half), F32),
             pltpu.VMEM((4, width, width), F32),
             pltpu.VMEM((4, width, width), F32),
-            pltpu.SemaphoreType.DMA((25,)),
-            pltpu.SemaphoreType.DMA((25,)),
+            pltpu.SemaphoreType.DMA((28,)),
+            pltpu.SemaphoreType.DMA((28,)),
         ],
         compiler_params=pltpu.CompilerParams(
             collective_id=0, has_side_effects=True, vmem_limit_bytes=48 * 1024 * 1024),

time: 174 us -> 126 us (0.72)
  Pallas kernels: 172 us -> 123 us
    pallas_call x1, Pallas kernels: 172 us -> 123 us  [fused(): pl.pallas_call(kernel, out_shape=jax.ShapeDtypeStruct((rows, 4 * width),...]
where the time goes in v2:
time: 126 us; the launch traced here: 125 us
  Pallas kernels  123 us (98%)
  local copies, waits for them, and re-layouts  2.02 us (2%)
    pallas_call x1, Pallas kernels, fused(): pl.pallas_call(kernel, out_shape=jax.ShapeDtypeStruct((rows, 4 * width),...  123 us

profile of v2, /device:TPU:0, one launch (start us, length us, event | category | flops | bytes accessed | tf_op | source)
XLA Modules:
  0.0 125.3 jit_solution(5194497988472803773)
XLA Ops:
  0.0 123.3 %shard_map.17 = f32[1024,1024]{1,0:T(8,128)S(1)} custom-call(f32[4096,256]{1,0:T(8,128)} %x_ref.1), custom_call_target="tpu_custom_call" | custom-call | tf_op jit(solution)/shard_map/pallas_call | solution.py:286
  123.3 2.0 %copy.3 = f32[1,1024,1024]{2,1,0:T(8,128)} copy(f32[1,1024,1024]{2,1,0:T(8,128)S(1)} %bitcast.1) | data formatting | bytes 8388608

commit v3 on v2

--- a/solution.py
+++ b/solution.py
@@ -69,8 +69,8 @@
         z_ref[i] = exact_dot(middle, z_ref[i])
 
 
-def kernel(x_ref, out_ref, w, got, ex, g, ga, sb, gb, gf, y1, z1, dg, dq, df, part, rs, zb, cq, cf, y2, z2,
-           send_sem, recv_sem):
+def kernel(x_any, out_ref, x_ref, w, got, ex, g, ga, sb, gb, gf, y1, z1, dg, dq, df, part, rs, zb, cq, cf, y2, z2,
+           send_sem, recv_sem, load_sem):
     n_col, n_row = 4, 4
     c = lax.axis_index("col")
     r = lax.axis_index("row")
@@ -93,18 +93,27 @@
         copy.start()
         return copy
 
+    tile = slab // 8
+
+    def load(t):
+        at = pl.ds(pl.multiple_of(t * tile, tile), tile)
+        return pltpu.make_async_copy(x_any.at[at], x_ref.at[at], load_sem.at[t])
+
+    for t in range(8):
+        load(t).start()
+
     barrier = pltpu.get_barrier_semaphore()
     for k in range(1, n_row):
         pl.semaphore_signal(barrier, inc=1, device_id=row_peer(k), device_id_type=MESH)
     for k in range(1, n_col):
         pl.semaphore_signal(barrier, inc=1, device_id=col_peer(k), device_id_type=MESH)
 
-    tile = 512
     g[...] = jnp.zeros_like(g)
     gf[...] = jnp.zeros_like(gf)
 
     @pl.loop(0, slab // tile)
     def _(t):
+        load(t).wait()
         piece = halves_of(x_ref[pl.ds(pl.multiple_of(t * tile, tile), tile), :])
         g[...] += lax.dot_general(piece[0], piece[0], ROWS_FIRST, preferred_element_type=F32)
         gf[...] += lax.dot_general(piece[0], piece[1], ROWS_FIRST, preferred_element_type=F32)
@@ -185,8 +194,6 @@
             sent.append(remote(w.at[ho, at], got.at[c, ho, to], sem + i, {"col": j}))
         return sent
 
-    for copy in crossing:
-        copy.wait_send()
     second = later(0, 14)
 
     for copy in diagonal:
@@ -197,7 +204,7 @@
     for copy in diagonal[3:]:
         copy.wait()
     for copy in crossing:
-        copy.wait_recv()
+        copy.wait()
     for copy in near:
         copy.wait()
 
@@ -286,9 +293,10 @@
     out = pl.pallas_call(
         kernel,
         out_shape=jax.ShapeDtypeStruct((rows, 4 * width), F32),
-        in_specs=[pl.BlockSpec(memory_space=pltpu.VMEM)],
+        in_specs=[pl.BlockSpec(memory_space=pl.ANY)],
         out_specs=pl.BlockSpec(memory_space=pltpu.VMEM),
         scratch_shapes=[
+            pltpu.VMEM((slab, width), F32),
             pltpu.VMEM((2, slab, half), F32),
             pltpu.VMEM((4, 2, rows, half), F32),
             pltpu.VMEM((2, rows, half), F32),
@@ -311,6 +319,7 @@
             pltpu.VMEM((4, width, width), F32),
             pltpu.SemaphoreType.DMA((28,)),
             pltpu.SemaphoreType.DMA((28,)),
+            pltpu.SemaphoreType.DMA((8,)),
         ],
         compiler_params=pltpu.CompilerParams(
             collective_id=0, has_side_effects=True, vmem_limit_bytes=48 * 1024 * 1024),

time: 126 us -> 131 us (1.040)
  Pallas kernels: 123 us -> 129 us
    pallas_call x1, Pallas kernels: 123 us -> 129 us  [fused(): pl.pallas_call(kernel, out_shape=jax.ShapeDtypeStruct((rows, 4 * width),...]
where the time goes in v3:
time: 131 us
  Pallas kernels  129 us (98%)
  local copies, waits for them, and re-layouts  2.02 us (2%)
    pallas_call x1, Pallas kernels, fused(): pl.pallas_call(kernel, out_shape=jax.ShapeDtypeStruct((rows, 4 * width),...  129 us

profile of v3, /device:TPU:0, one launch (start us, length us, event | category | flops | bytes accessed | tf_op | source)
XLA Modules:
  0.0 130.7 jit_solution(313375887672145042)
XLA Ops:
  0.0 128.6 %shard_map.17 = f32[1024,1024]{1,0:T(8,128)S(1)} custom-call(f32[4096,256]{1,0:T(8,128)} %x_any.1), custom_call_target="tpu_custom_call" | custom-call | tf_op jit(solution)/shard_map/pallas_call | solution.py:293
  128.6 2.0 %copy.3 = f32[1,1024,1024]{2,1,0:T(8,128)} copy(f32[1,1024,1024]{2,1,0:T(8,128)S(1)} %bitcast.1) | data formatting | bytes 8388608

commit v4 on v3

--- a/solution.py
+++ b/solution.py
@@ -194,6 +194,8 @@
             sent.append(remote(w.at[ho, at], got.at[c, ho, to], sem + i, {"col": j}))
         return sent
 
+    for copy in crossing:
+        copy.wait_send()
     second = later(0, 14)
 
     for copy in diagonal:
@@ -204,7 +206,7 @@
     for copy in diagonal[3:]:
         copy.wait()
     for copy in crossing:
-        copy.wait()
+        copy.wait_recv()
     for copy in near:
         copy.wait()
 

time: 131 us -> 131 us (level)
  no operation moved by 1% of the time
where the time goes in v4:
time: 131 us
  Pallas kernels  129 us (98%)
  local copies, waits for them, and re-layouts  2.02 us (2%)
    pallas_call x1, Pallas kernels, fused(): pl.pallas_call(kernel, out_shape=jax.ShapeDtypeStruct((rows, 4 * width),...  129 us

profile of v4, /device:TPU:0, one launch (start us, length us, event | category | flops | bytes accessed | tf_op | source)
XLA Modules:
  0.0 130.7 jit_solution(1827684699824869900)
XLA Ops:
  0.0 128.6 %shard_map.17 = f32[1024,1024]{1,0:T(8,128)S(1)} custom-call(f32[4096,256]{1,0:T(8,128)} %x_any.1), custom_call_target="tpu_custom_call" | custom-call | tf_op jit(solution)/shard_map/pallas_call | solution.py:295
  128.6 2.0 %copy.3 = f32[1,1024,1024]{2,1,0:T(8,128)} copy(f32[1,1024,1024]{2,1,0:T(8,128)S(1)} %bitcast.1) | data formatting | bytes 8388608
